TPU v7x, 256 devices: a whole 4x4x8 slice. The times are simulated.
256 devices in a mesh: replica: 16 (over y, z_lo), shard: 16 (over z_hi, x, core).
Axes of the slice: x: 4, y: 4, z: 8 (z_hi: 2, z_lo: 4; z = z_hi * 4 + z_lo), core: 2. Of those that a mesh axis runs over, the one named last changes fastest.
Arguments:
- outer_weight: float32 [16, 5120, 2048], P('replica', 'shard'), may hold values from -0.078125 to 0.078125
- inner_weight: bfloat16 [16, 5120, 2048], P('replica', 'shard'), may hold values from -0.078125 to 0.078125
- momentum: bfloat16 [16, 5120, 2048], P('replica', 'shard'), may hold values from -0.0390625 to 0.0390625
- matching: int32 [16], replicated, may hold values from 0 to 15, each once
- tokens: bfloat16 [16, 4096, 5120], P('replica', 'shard'), may hold values from -6 to 6
- norm_gain: float32 [16, 5120], P('replica'), may hold values from 0.1 to 1.9
- kv_bias: float32 [16, 2048], P('replica'), may hold values from -3 to 3
Outputs:
- new_outer: float32 [16, 5120, 2048], P('replica', 'shard')
- new_momentum: bfloat16 [16, 5120, 2048], P('replica', 'shard')
- keys_values: bfloat16 [16, 4096, 2048], P('replica', 'shard')
Inputs may be any that keep to these rules, and one draw needn't show every extreme that they name: Replicas matching[2k] and matching[2k+1] are partners; every replica appears exactly once.
All inputs are finite; a program needn't handle non-finite values.
Results may differ from a plain program's by a relative error of at most 0.0074.
Values may be sent and summed in bfloat16 or wider, within the bound.
A program may use at most 128 MiB of HBM per device.

v0:
```python
import jax
import jax.numpy as jnp
from jax import lax
from jax.sharding import PartitionSpec as P

KV_HEADS = 8
HEAD_DIM = 128


momentum_rate = 0.9
outer_rate = 0.7
gossip_rate = 0.5
norm_eps = 1e-06
rope_base = 1000000.0


def partner_table(matching):
    total_count = matching.shape[0]
    indices = jnp.arange(total_count, dtype=jnp.int32)
    matches = (matching[None, :] == indices[:, None]).astype(jnp.int32)
    position = jnp.sum(matches * indices[None, :], axis=1)
    mate_pos = position + 1 - 2 * (position % 2)
    picked = (indices[None, :] == mate_pos[:, None]).astype(jnp.int32)
    return jnp.sum(picked * matching[None, :], axis=1)


def rms_normed(token_rows, gain):
    values = token_rows.astype(jnp.float32)
    mean_square = jnp.mean(values * values, axis=-1, keepdims=True)
    return (values * lax.rsqrt(mean_square + norm_eps) * gain[None, :]).astype(jnp.bfloat16)


def rotary(projected, positions):
    tok_count = projected.shape[0]
    key_width = KV_HEADS * HEAD_DIM
    half_dim = HEAD_DIM // 2
    exponents = jnp.arange(half_dim, dtype=jnp.float32) * (2.0 / HEAD_DIM)
    inverse = rope_base ** (-exponents)
    angles = positions[:, None] * inverse[None, :]
    cosine = jnp.cos(angles)[:, None, :]
    sine_vals = jnp.sin(angles)[:, None, :]
    key_cols = projected[:, :key_width].reshape(tok_count, KV_HEADS, HEAD_DIM)
    first_half = key_cols[..., :half_dim]
    second_half = key_cols[..., half_dim:]
    turned = jnp.concatenate(
        [
            first_half * cosine - second_half * sine_vals,
            second_half * cosine + first_half * sine_vals,
        ],
        axis=-1,
    )
    return jnp.concatenate([turned.reshape(tok_count, key_width), projected[:, key_width:]], axis=1)


def accumulate(arranged, shard_piece):
    return jnp.dot(arranged, shard_piece, preferred_element_type=jnp.float32)


def on_device(outer_weight, inner_weight, momentum, matching, tokens, norm_gain, kv_bias):
    outer_rows = outer_weight[0]
    inner_rows = inner_weight[0]
    moment_rows = momentum[0]
    rows_here = outer_rows.shape[0]
    tok_count = tokens.shape[1]
    shards = lax.axis_size("shard")
    partner = partner_table(matching)
    normed = rms_normed(tokens[0], norm_gain[0])
    blocks = 1
    block_rows = rows_here // blocks
    own_delta = (outer_rows - inner_rows.astype(jnp.float32)).astype(jnp.bfloat16)
    own_round = outer_rows.astype(jnp.bfloat16)
    got_delta = lax.all_to_all(
        own_delta[None], "replica", split_axis=2, concat_axis=0, tiled=True
    ).astype(jnp.float32)
    got_outer = lax.all_to_all(
        own_round[None], "replica", split_axis=2, concat_axis=0, tiled=True
    ).astype(jnp.float32)
    pair_delta = ((got_delta + jnp.take(got_delta, partner, axis=0)) * 0.5).astype(jnp.bfloat16)
    pair_outer = ((got_outer + jnp.take(got_outer, partner, axis=0)) * 0.5).astype(jnp.bfloat16)
    pair_delta, pair_outer = (
        lax.all_to_all(pair_delta, "replica", split_axis=0, concat_axis=2, tiled=True),
        lax.all_to_all(pair_outer, "replica", split_axis=0, concat_axis=2, tiled=True),
    )
    pair_delta = pair_delta[0].astype(jnp.float32)
    pair_outer = pair_outer[0].astype(jnp.float32)
    velocity = momentum_rate * moment_rows.astype(jnp.float32) + pair_delta
    updated = (
        outer_rows
        - outer_rate * (pair_delta + momentum_rate * velocity)
        - gossip_rate * (outer_rows - pair_outer)
    )
    moment_parts = velocity.astype(jnp.bfloat16)
    arranged = normed.reshape(tok_count, shards, blocks, block_rows)[:, :, 0, :].reshape(
        tok_count, shards * block_rows
    )
    running = accumulate(
        arranged, lax.all_gather(updated.astype(jnp.bfloat16), "shard", axis=0, tiled=True)
    )
    positions = (
        lax.axis_index("shard") * tok_count + jnp.arange(tok_count, dtype=jnp.int32)
    ).astype(jnp.float32)
    projected = running + kv_bias[0][None, :]
    keys_values = rotary(projected, positions).astype(jnp.bfloat16)
    return (updated[None], moment_parts[None], keys_values[None])


def solution(mesh):
    in_specs = (
        P("replica", "shard", None),
        P("replica", "shard", None),
        P("replica", "shard", None),
        P(),
        P("replica", "shard", None),
        P("replica", None),
        P("replica", None),
    )
    out_specs = (
        P("replica", "shard", None),
        P("replica", "shard", None),
        P("replica", "shard", None),
    )
    return jax.shard_map(
        on_device, mesh=mesh, in_specs=in_specs, out_specs=out_specs, check_vma=False
    )
```

profile of v0, /device:TPU:1, one launch (start us, length us, event | category | flops | bytes accessed | tf_op | source)
XLA Modules:
  0.0 503.5 jit_solution(10274361575701660835)
XLA Ops:
  7.2 5.0 subtract_convert_fusion
  12.2 7.8 %copy.53 = bf16[1,320,2048]{1,0,2:T(2,128)(2,1)S(1)} copy(bf16[1,320,2048]{2,1,0:T(8,128)(2,1)} %get-tuple-element.15) | data formatting | bytes 2621440 | tf_op jit(solution)/shard_map/convert_element_type | solution.py:70
  20.0 0.5 broadcast.162
  20.5 34.5 %reduce = bf16[2048,320]{1,0:T(8,128)(2,1)} reduce(bf16[2048,1,320]{2,1,0:T(2,128)(2,1)S(1)} %bitcast.90, bf16[]{:T(256)} %broadcast.162), dimensions={1}, to_apply=%bitcast.81.reduce_sub_computation | reduce | bytes 2621442
  55.0 4.8 reshape.220
  59.8 9.5 %all-to-all-start = ((bf16[16,2,20480]{2,1,0:T(2,128)(2,1)}), bf16[16,2,20480]{2,1,0:T(2,128)(2,1)}, u32[]{:S(2)}, u32[]{:S(2)}) async-start(bf16[16,2,20480]{2,1,0:T(2,128)(2,1)} %reshape.220), calls=%async_computation | async-start | bytes 2621440 | tf_op jit(solution)/shard_map/all_to_all | solution.py:72
  69.3 7.8 %copy.59 = bf16[1,320,2048]{1,0,2:T(2,128)(2,1)S(1)} copy(bf16[1,320,2048]{2,1,0:T(8,128)(2,1)} %get-tuple-element.16) | data formatting | bytes 2621440 | tf_op jit(solution)/shard_map/convert_element_type | solution.py:71
  77.2 34.5 %reduce.1 = bf16[2048,320]{1,0:T(8,128)(2,1)} reduce(bf16[2048,1,320]{2,1,0:T(2,128)(2,1)S(1)} %bitcast.91, bf16[]{:T(256)} %broadcast.162), dimensions={1}, to_apply=%bitcast.79.reduce_sub_computation | reduce | bytes 2621442
  111.6 4.8 reshape.218
  116.5 7.6 %all-to-all-start.2 = ((bf16[16,2,20480]{2,1,0:T(2,128)(2,1)}), bf16[16,2,20480]{2,1,0:T(2,128)(2,1)}, u32[]{:S(2)}, u32[]{:S(2)}) async-start(bf16[16,2,20480]{2,1,0:T(2,128)(2,1)} %reshape.218), calls=%async_computation.2 | async-start | bytes 2621440 | tf_op jit(solution)/shard_map/all_to_all | solution.py:75
  124.5 8.9 %reshape.221 = bf16[2048,1,320]{2,1,0:T(2,128)(2,1)S(1)} reshape(bf16[16,2,20480]{2,1,0:T(2,128)(2,1)} %all-to-all-done) | data formatting | bytes 2621440
  133.3 6.1 %copy.54 = bf16[1,320,2048]{2,1,0:T(8,128)(2,1)} copy(bf16[1,320,2048]{1,0,2:T(2,128)(2,1)S(1)} %bitcast.92) | data formatting | bytes 2621440 | tf_op jit(solution)/shard_map/all_to_all | solution.py:72
  139.4 1.6 convert_bitcast_fusion.3
  141.0 0.5 copy.66
  141.6 2.3 copy.87
  143.9 12.9 %all-to-all-done.2 = bf16[16,2,20480]{2,1,0:T(2,128)(2,1)} async-done(((bf16[16,2,20480]{2,1,0:T(2,128)(2,1)}), bf16[16,2,20480]{2,1,0:T(2,128)(2,1)}, u32[]{:S(2)}, u32[]{:S(2)}) %all-to-all-start.2) | async-done | bytes 1310752 | tf_op jit(solution)/shard_map/all_to_all | solution.py:75
  156.8 10.5 %reshape.219 = bf16[2048,1,320]{2,1,0:T(2,128)(2,1)} reshape(bf16[16,2,20480]{2,1,0:T(2,128)(2,1)} %all-to-all-done.2) | data formatting | bytes 2621440
  167.2 8.1 %copy.60 = bf16[1,320,2048]{2,1,0:T(8,128)(2,1)} copy(bf16[1,320,2048]{1,0,2:T(2,128)(2,1)} %bitcast.93) | data formatting | bytes 2621440 | tf_op jit(solution)/shard_map/all_to_all | solution.py:75
  175.4 1.6 convert_bitcast_fusion.2
  177.0 0.5 copy.67
  177.5 2.3 copy.86
  179.8 4.0 gather_fusion
  183.8 3.9 gather_fusion.1
  187.7 6.5 %fusion.16 = (bf16[16,320,128]{2,1,0:T(8,128)(2,1)}, bf16[16,320,128]{2,1,0:T(8,128)(2,1)S(1)}) fusion(f32[16,320,128]{2,1,0:T(8,128)} %gather_fusion, pred[16]{0:T(512)(128)(4,1)S(1)} %compare_and_fusion, f32[1,320,16,128]{3,2,0,1:T(8,128)S(1)} %bitcast.87, f32[16,320,128]{2,1,0:T(8,128)} %gather_fusion.1, f32[1,320,16,128]{3,2,0,1:T(8,128)} %bitcast.89), kind=kLoop, calls=%fused_computation.30 | loop fusion | flops 5242880 | bytes 13107216 | tf_op jit(solution)/shard_map/convert_element_type | solution.py:78
  194.2 37.2 %all_to_all.16 = bf16[16,320,128]{2,1,0:T(8,128)(2,1)S(1)} all-to-all(bf16[16,320,128]{2,1,0:T(8,128)(2,1)S(1)} %get-tuple-element.22), channel_id=1, replica_groups=mesh['replica'=16,'shard'=16] {'replica'}, dimensions={0} | all-to-all | bytes 2621440 | tf_op jit(solution)/shard_map/all_to_all | solution.py:82
  231.4 3.7 all-to-all-start.1
  235.1 0.2 all-gather.2.cloned.1.call-start
  235.3 0.3 convert_bitcast_fusion
  235.6 1.5 copy-done.2
  237.1 3.0 copy.65
  240.2 27.5 %all-to-all-done.1 = bf16[16,320,128]{2,1,0:T(8,128)(2,1)S(1)} async-done(((bf16[16,320,128]{2,1,0:T(8,128)(2,1)}), bf16[16,320,128]{2,1,0:T(8,128)(2,1)S(1)}, u32[]{:S(2)}, u32[]{:S(2)}) %all-to-all-start.1) | async-done | bytes 1310752 | tf_op jit(solution)/shard_map/all_to_all | solution.py:81
  267.7 0.2 convert_bitcast_fusion.1
  268.0 1.5 copy.64
  269.5 1.2 copy-done
  270.8 0.8 copy-done.6
  271.6 3.6 fusion.6
  275.2 2.5 fusion
  277.7 0.5 multiply_cosine_fusion
  278.2 1.5 copy.56
  279.8 0.2 copy-done.3
  280.0 1.5 copy.62
  281.5 5.2 %fusion.20 = (bf16[1,320,2048]{2,1,0:T(8,128)(2,1)}, f32[1,320,2048]{2,1,0:T(8,128)}) fusion(bf16[1,320,2048]{2,1,0:T(8,128)(2,1)S(1)} %copy-done.8, f32[1,320,2048]{2,0,1:T(1,128)S(1)} %bitcast.98, f32[1,320,2048]{2,1,0:T(8,128)S(1)} %copy-done, f32[1,320,2048]{2,0,1:T(1,128)S(1)} %bitcast.99), kind=kLoop, calls=%fused_computation.37 | loop fusion | flops 7208960 | bytes 13107200 | tf_op jit(solution)/shard_map/convert_element_type | solution.py:92
  286.7 196.5 %all-gather.2.cloned.1.call-done = bf16[5120,2048]{1,0:T(8,128)(2,1)} async-done(((bf16[320,2048]{1,0:T(8,128)(2,1)}), bf16[5120,2048]{1,0:T(8,128)(2,1)}) %all-gather.2.cloned.1.call-update) | async-done | bytes 20971536 | tf_op jit(solution)/shard_map/all_gather | solution.py:97
  483.3 10.7 %convolution_add_fusion = f32[256,2048]{1,0:T(8,128)S(1)} fusion(bf16[5120,2048]{1,0:T(8,128)(2,1)} %all-gather.2.cloned.1.call-done, bf16[1,256,5120]{2,1,0:T(8,128)(2,1)} %param.13, f32[5120]{0:T(1024)S(1)} %bitcast.101, f32[256]{0:T(256)S(1)} %add_rsqrt_fusion, f32[2048]{0:T(1024)S(1)} %bitcast.102), kind=kOutput, calls=%fused_computation.7 | convolution fusion | flops 5374476288 | bytes 25719808 | tf_op jit(solution)/shard_map/dot_general | solution.py:56
  494.3 0.5 subtract_convert_fusion.1
  494.8 0.3 pad_maximum_fusion.1
  495.1 0.2 concatenate.20
  495.3 1.1 pad_maximum_fusion
  (34 shorter events, 0.8 us)
Async XLA Ops:
  59.8 56.7 %all-to-all-start = ((bf16[16,2,20480]{2,1,0:T(2,128)(2,1)}), bf16[16,2,20480]{2,1,0:T(2,128)(2,1)}, u32[]{:S(2)}, u32[]{:S(2)}) async-start(bf16[16,2,20480]{2,1,0:T(2,128)(2,1)} %reshape.220), calls=%async_computation | async-start | bytes 2621440 | tf_op jit(solution)/shard_map/all_to_all | solution.py:72
  111.6 12.5 %copy-start.11 = (s32[16]{0:T(128)S(1)}, s32[16]{0:T(128)}, u32[]{:S(2)}) copy-start(s32[16]{0:T(128)} %param.12) | copy-start | bytes 196
  116.5 40.3 %all-to-all-start.2 = ((bf16[16,2,20480]{2,1,0:T(2,128)(2,1)}), bf16[16,2,20480]{2,1,0:T(2,128)(2,1)}, u32[]{:S(2)}, u32[]{:S(2)}) async-start(bf16[16,2,20480]{2,1,0:T(2,128)(2,1)} %reshape.218), calls=%async_computation.2 | async-start | bytes 2621440 | tf_op jit(solution)/shard_map/all_to_all | solution.py:75
  177.5 2.3 copy-start.1
  231.4 36.3 %all-to-all-start.1 = ((bf16[16,320,128]{2,1,0:T(8,128)(2,1)}), bf16[16,320,128]{2,1,0:T(8,128)(2,1)S(1)}, u32[]{:S(2)}, u32[]{:S(2)}) async-start(bf16[16,320,128]{2,1,0:T(8,128)(2,1)} %get-tuple-element.21), calls=%async_computation.1 | async-start | bytes 2621440 | tf_op jit(solution)/shard_map/all_to_all | solution.py:81
  235.1 248.2 %all-gather.2.cloned.1.call-start = ((), (), s32[]{:S(2)}) async-start(), calls=%async_computation.4 | async-start | bytes 22282240 | tf_op jit(solution)/shard_map/all_gather | solution.py:97
  235.6 1.5 copy-start.2
  267.7 1.8 copy-start.7
  267.9 1.6 copy-start.4
  267.9 2.8 copy-start
  268.0 3.6 copy-start.6
  275.1 3.1 copy-start.5
  278.2 1.7 copy-start.3
  280.0 1.5 copy-start.8
  281.5 201.8 %copy-start.9 = (f32[1,5120]{1,0:T(1,128)S(1)}, f32[1,5120]{1,0:T(1,128)}, u32[]{:S(2)}) copy-start(f32[1,5120]{1,0:T(1,128)} %param.14) | copy-start | bytes 61444
  281.5 201.7 %copy-start.10 = (f32[1,2048]{1,0:T(1,128)S(1)}, f32[1,2048]{1,0:T(1,128)}, u32[]{:S(2)}) copy-start(f32[1,2048]{1,0:T(1,128)} %param.15) | copy-start | bytes 24580
Sparse Core Ops, SparseCore 0:
  275.3 207.9 all-gather.1
where the time goes:
time: 512 us; the launch traced here: 503 us
  waiting for transfers between devices  237 us (46%)
  other arithmetic  98.2 us (19%)
  local copies, waits for them, and re-layouts  84.9 us (17%)
  blocking collectives  37.2 us (7%)
  starting transfers between devices  21.1 us (4%)
  between operations  14.6 us (3%)
  matrix products  10.7 us (2%)
    all_gather x1, waiting for transfers between devices, on_device(): lax.all_gather(updated.astype(jnp.bfloat16), 'shard', axis=0, tiled=True)  197 us
    unnamed x4, other arithmetic  72.2 us
    all_to_all x1, blocking collectives, on_device(): lax.all_to_all(pair_outer, 'replica', split_axis=0, concat_axis=2, tiled=...  37.2 us
    unnamed x33, local copies, waits for them, and re-layouts  34.6 us
    all_to_all x1, waiting for transfers between devices, on_device(): lax.all_to_all(pair_delta, 'replica', split_axis=0, concat_axis=2, tiled=...  27.5 us
    all_to_all x1, waiting for transfers between devices, on_device(): lax.all_to_all(own_round[None], 'replica', split_axis=2, concat_axis=0, t...  12.9 us
    dot_general x1, matrix products, accumulate(): return jnp.dot(arranged, shard_piece, preferred_element_type=jnp.float32)  10.7 us
  transfers between devices with their start and end apart: 4, of which 3 were waited for; matrix products, arithmetic and copies ran while one was open for 16% of the time, Pallas kernels for 0%

commit v1 on v0

v1 whole, which is shorter than its diff:
```python
import functools

import jax
import jax.numpy as jnp
from jax import lax
from jax.experimental import pallas as pl
from jax.experimental.pallas import tpu as pltpu
from jax.sharding import PartitionSpec as P

MESH = pl.DeviceIdType.MESH
BF16 = jnp.bfloat16
F32 = jnp.float32

HEAD_DIM = 128
KEY_WIDTH = 1024
momentum_rate = 0.9
outer_rate = 0.7
gossip_rate = 0.5
norm_eps = 1e-06
rope_base = 1000000.0

ROWS = 320
WIDTH = 2048
TOKENS = 256
DEPTH = 5120
GROUP = ROWS // 4
HALF = ROWS // 2
CHUNKS = 8
CW = WIDTH // CHUNKS
AHEAD = 2
NORM_TICKS = 4

A, B, C, D, X1, X2, F1, F2, K = range(9)
SA, SB, SC, SW = range(4)
LO, LI, OO, OM, OK = range(5)


def kernel(
    slots,
    mate_ref,
    outer_hbm,
    inner_hbm,
    moment_hbm,
    token_hbm,
    gain_ref,
    bias_ref,
    cos_ref,
    sin_ref,
    new_outer_hbm,
    new_moment_hbm,
    kv_hbm,
    outer,
    inner,
    moment,
    normed,
    sent,
    pool,
    crossing,
    means,
    pair,
    weights,
    kv,
    recv,
    send,
    local,
    single,
):
    r, s = lax.axis_index("replica"), lax.axis_index("shard")
    y, zl = r // 4, r % 4
    zh, x, core = s // 8, (s // 2) % 4, s % 2
    side = zl // 2
    hub_z = 1 + side
    is_hub = zl == hub_z
    far = 3 - zl
    edge = 3 * side

    def place(py, pz, ph, px, pc):
        return (py * 4 + pz, ph * 8 + px * 2 + pc)

    right, left = (x + 1) % 4, (x + 3) % 4
    to_core = place(y, zl, zh, x, 1 - core)
    to_right = place(y, zl, zh, right, core)
    to_left = place(y, zl, zh, left, core)
    to_far = place(y, zl, 1 - zh, x, core)

    def rows_of(ph, px, pc, start=0, size=ROWS):
        return pl.ds(pl.multiple_of((ph * 8 + px * 2 + pc) * ROWS + start, 16), size)

    def cols(n):
        return pl.ds(pl.multiple_of(n * CW, CW), CW)

    def remote(src, dst, ssem, rsem, device):
        pltpu.make_async_remote_copy(
            src_ref=src, dst_ref=dst, send_sem=ssem, recv_sem=rsem, device_id=device, device_id_type=MESH
        ).start()

    def taken(ref, sem):
        pltpu.make_async_copy(ref, ref, sem).wait()

    def loads(n):
        return (
            pltpu.make_async_copy(outer_hbm.at[:, cols(n)], outer.at[n], local.at[LO, n]),
            pltpu.make_async_copy(inner_hbm.at[:, cols(n)], inner.at[n], local.at[LI, n]),
        )

    def moment_load(n):
        return pltpu.make_async_copy(moment_hbm.at[:, cols(n)], moment.at[n], local.at[OM, n])

    token_load = pltpu.make_async_copy(token_hbm, normed, single.at[0])

    def start_loads(n, _):
        for copy in loads(n):
            copy.start()
        return 0

    lax.fori_loop(0, CHUNKS, start_loads, 0)
    token_load.start()

    def start_moment(n, _):
        moment_load(n).start()
        return 0

    lax.fori_loop(0, CHUNKS, start_moment, 0)

    barrier = pltpu.get_barrier_semaphore()

    def greet(device):
        pl.semaphore_signal(barrier, inc=1, device_id=device, device_id_type=MESH)

    for device in (to_core, to_right, to_left, to_far):
        greet(device)

    @pl.when(is_hub)
    def _():
        for step in range(4):
            greet(place((y + step) % 4, edge, zh, x, core))
        for step in range(1, 4):
            greet(place((y + step) % 4, zl, zh, x, core))
        greet(place(y, far, zh, x, core))
        pl.semaphore_wait(barrier, 12)

    @pl.when(jnp.logical_not(is_hub))
    def _():
        for step in range(4):
            greet(place((y + step) % 4, hub_z, zh, x, core))
        pl.semaphore_wait(barrier, 8)

    item = (zl % 2) * 4 + y

    def send_rows(n):
        for copy in loads(n):
            copy.wait()

        def group(g, _):
            rows = pl.ds(pl.multiple_of(g * GROUP, 16), GROUP)
            own = outer[n, rows, :]
            sent[n, g, 0] = (own - inner[n, rows, :].astype(F32)).astype(BF16)
            sent[n, g, 1] = own.astype(BF16)
            return 0

        lax.fori_loop(0, 4, group, 0)
        for step in range(4):
            to_y = (y + step) % 4
            src, dst = sent.at[n, to_y], pool.at[n, item]
            if step:
                remote(src, dst, send.at[SA, n], recv.at[A, n], place(to_y, hub_z, zh, x, core))
            else:

                @pl.when(is_hub)
                def _():
                    pltpu.make_async_copy(src, dst, recv.at[A, n]).start()

                @pl.when(jnp.logical_not(is_hub))
                def _():
                    remote(src, dst, send.at[SA, n], recv.at[A, n], place(to_y, hub_z, zh, x, core))

    def swap_sides(n):
        taken(pool.at[n, pl.ds(0, 8)], recv.at[A, n])
        if slots < 8:

            def part(i, _):
                v = i // 5
                rows = pl.ds(pl.multiple_of((i % 5) * 16, 16), 16)
                held = [pool[n, j, v, rows, :] for j in range(8)]
                for k in range(slots):
                    which = mate_ref[16 + side * 8 + k]
                    value = held[0]
                    for j in range(1, 8):
                        value = jnp.where(which == j, held[j], value)
                    crossing[n, k, v, rows, :] = value
                return 0

            lax.fori_loop(0, 10, part, 0)
            src = crossing.at[n]
        else:
            src = pool.at[n, pl.ds(0, 8)]
        remote(src, pool.at[n, pl.ds(8, slots)], send.at[SB, n], recv.at[B, n], place(y, far, zh, x, core))

    def average(n):
        taken(pool.at[n, pl.ds(8, slots)], recv.at[B, n])
        mates = [mate_ref[side * 8 + k] for k in range(8)]

        def part(i, _):
            v = i // 5
            rows = pl.ds(pl.multiple_of((i % 5) * 16, 16), 16)
            held = [pool[n, j, v, rows, :] for j in range(8 + slots)]
            for k in range(8):
                value = held[0]
                for j in range(1, 8 + slots):
                    value = jnp.where(mates[k] == j, held[j], value)
                means[n, k, v, rows, :] = ((held[k].astype(F32) + value.astype(F32)) * 0.5).astype(BF16)
            return 0

        lax.fori_loop(0, 10, part, 0)
        for step in range(4):
            to_y = (y + step) % 4
            src, dst = means.at[n, (zl % 2) * 4 + to_y], pair.at[n, y]
            if step:
                remote(src, dst, send.at[SC, n], recv.at[C, n], place(to_y, zl, zh, x, core))
            else:
                pltpu.make_async_copy(src, dst, recv.at[C, n]).start()
            remote(
                means.at[n, (edge % 2) * 4 + to_y],
                dst,
                send.at[SC, n],
                recv.at[C, n],
                place(to_y, edge, zh, x, core),
            )

    def pass_on(n, rows, rsem, device):
        block = weights.at[n, rows]
        remote(block, block, send.at[SW, n], recv.at[rsem, n], device)

    def update(n):
        taken(pair.at[n], recv.at[C, n])
        moment_load(n).wait()

        def group(g, _):
            rows = pl.ds(pl.multiple_of(g * GROUP, 16), GROUP)
            own = outer[n, rows, :]
            delta = pair[n, g, 0].astype(F32)
            velocity = momentum_rate * moment[n, rows, :].astype(F32) + delta
            updated = (
                own
                - outer_rate * (delta + momentum_rate * velocity)
                - gossip_rate * (own - pair[n, g, 1].astype(F32))
            )
            outer[n, rows, :] = updated
            moment[n, rows, :] = velocity.astype(BF16)
            weights[n, pl.ds(pl.multiple_of(s * ROWS + g * GROUP, 16), GROUP), :] = updated.astype(BF16)
            return 0

        lax.fori_loop(0, 4, group, 0)
        own_rows = rows_of(zh, x, core)
        pass_on(n, own_rows, D, to_far)
        pass_on(n, own_rows, X1, to_right)
        pass_on(n, own_rows, X1, to_left)
        pass_on(n, own_rows, K, to_core)
        outer_store(n).start()
        moment_store(n).start()

    def outer_store(n):
        return pltpu.make_async_copy(outer.at[n], new_outer_hbm.at[:, cols(n)], local.at[OO, n])

    def moment_store(n):
        return pltpu.make_async_copy(moment.at[n], new_moment_hbm.at[:, cols(n)], local.at[OM, n])

    def kv_store(n):
        return pltpu.make_async_copy(kv.at[n], kv_hbm.at[:, cols(n)], local.at[OK, n])

    def forward(n, ph, rsem):
        pass_on(n, rows_of(ph, left, core, 0, HALF), rsem, to_right)
        pass_on(n, rows_of(ph, right, core, HALF, HALF), rsem, to_left)
        pass_on(n, rows_of(ph, left, core), K, to_core)
        pass_on(n, rows_of(ph, right, core), K, to_core)

    def first_hop(n):
        taken(weights.at[n, rows_of(1 - zh, x, core)], recv.at[D, n])
        far_rows = rows_of(1 - zh, x, core)
        pass_on(n, far_rows, X2, to_right)
        pass_on(n, far_rows, X2, to_left)
        pass_on(n, far_rows, K, to_core)
        taken(weights.at[n, pl.ds(0, 2 * ROWS)], recv.at[X1, n])
        forward(n, zh, F1)

    def second_hop(n):
        taken(weights.at[n, pl.ds(0, 2 * ROWS)], recv.at[X2, n])
        forward(n, 1 - zh, F2)
        taken(weights.at[n, pl.ds(0, ROWS)], recv.at[F1, n])
        pass_on(n, rows_of(zh, (x + 2) % 4, core), K, to_core)

    def third_hop(n):
        taken(weights.at[n, pl.ds(0, ROWS)], recv.at[F2, n])
        pass_on(n, rows_of(1 - zh, (x + 2) % 4, core), K, to_core)

    def norm_rows(t):
        @pl.when(t == 0)
        def _():
            token_load.wait()

        per_tick = TOKENS // NORM_TICKS

        def part(i, _):
            rows = pl.ds(pl.multiple_of(t * per_tick + i * 16, 16), 16)
            values = normed[rows, :].astype(F32)
            mean_square = jnp.mean(values * values, axis=-1, keepdims=True)
            normed[rows, :] = (values * lax.rsqrt(mean_square + norm_eps) * gain_ref[...]).astype(BF16)
            return 0

        lax.fori_loop(0, per_tick // 16, part, 0)

    def project(n):
        taken(weights.at[n, pl.ds(0, DEPTH // 2)], recv.at[K, n])
        out = jnp.dot(normed[...], weights[n], preferred_element_type=F32) + bias_ref[:, cols(n)]

        @pl.when(n * CW < KEY_WIDTH)
        def _():
            for h in range(CW // HEAD_DIM):
                head = out[:, h * HEAD_DIM : (h + 1) * HEAD_DIM]
                turned = head * cos_ref[...] + pltpu.roll(head, HEAD_DIM // 2, 1) * sin_ref[...]
                kv[n, :, h * HEAD_DIM : (h + 1) * HEAD_DIM] = turned.astype(BF16)

        @pl.when(n * CW >= KEY_WIDTH)
        def _():
            kv[n] = out.astype(BF16)

        kv_store(n).start()

    def first_rows(n, _):
        send_rows(n)
        return 0

    lax.fori_loop(0, AHEAD, first_rows, 0)

    def tick(t, _):
        @pl.when(t + AHEAD < CHUNKS)
        def _():
            send_rows(t + AHEAD)

        @pl.when(jnp.logical_and(is_hub, t < CHUNKS))
        def _():
            swap_sides(t)

        @pl.when(t < NORM_TICKS)
        def _():
            norm_rows(t)

        def staged(lag, stage, also=None):
            ready = jnp.logical_and(t >= lag, t < CHUNKS + lag)

            @pl.when(ready if also is None else jnp.logical_and(ready, also))
            def _():
                stage(t - lag)

        staged(1, average, is_hub)
        staged(2, update)
        staged(3, first_hop)
        staged(4, second_hop)
        staged(5, third_hop)
        staged(6, project)
        return 0

    lax.fori_loop(0, CHUNKS + 6, tick, 0)

    def drain(n, _):
        @pl.when(is_hub)
        def _():
            taken(sent.at[n, pl.ds(0, 3)], send.at[SA, n])
            taken(pool.at[n, pl.ds(8, slots)], send.at[SB, n])
            taken(means.at[n, pl.ds(0, 7)], send.at[SC, n])

        @pl.when(jnp.logical_not(is_hub))
        def _():
            taken(sent.at[n], send.at[SA, n])

        taken(weights.at[n, pl.ds(0, 15 * ROWS)], send.at[SW, n])
        outer_store(n).wait()
        moment_store(n).wait()
        kv_store(n).wait()
        return 0

    lax.fori_loop(0, CHUNKS, drain, 0)


def partner_table(matching):
    total_count = matching.shape[0]
    indices = jnp.arange(total_count, dtype=jnp.int32)
    matches = (matching[None, :] == indices[:, None]).astype(jnp.int32)
    position = jnp.sum(matches * indices[None, :], axis=1)
    mate_pos = position + 1 - 2 * (position % 2)
    picked = (indices[None, :] == mate_pos[:, None]).astype(jnp.int32)
    return jnp.sum(picked * matching[None, :], axis=1)


def on_device(outer_weight, inner_weight, momentum, matching, tokens, norm_gain, kv_bias):
    partner = partner_table(matching)
    order = jnp.arange(16, dtype=jnp.int32)
    replica_of = (order % 4) * 4 + (order // 8) * 2 + (order // 4) % 2
    mate = jnp.sum(jnp.where(replica_of[:, None] == jnp.arange(16)[None, :], partner[None, :], 0), axis=1)
    mate_item = (mate % 4) // 2 * 8 + (mate % 2) * 4 + mate // 4
    same_side = mate_item // 8 == order // 8
    table = jnp.where(same_side, mate_item % 8, 8 + mate_item % 8).astype(jnp.int32)

    positions = (lax.axis_index("shard") * TOKENS + jnp.arange(TOKENS, dtype=jnp.int32)).astype(F32)
    exponents = jnp.arange(HEAD_DIM // 2, dtype=F32) * (2.0 / HEAD_DIM)
    angles = positions[:, None] * (rope_base ** (-exponents))[None, :]
    cosine, sine = jnp.cos(angles), jnp.sin(angles)
    cosine = jnp.concatenate([cosine, cosine], axis=1)
    sine = jnp.concatenate([-sine, sine], axis=1)

    slots = 8
    hbm = pl.BlockSpec(memory_space=pl.ANY)
    vmem = pl.BlockSpec(memory_space=pltpu.VMEM)
    smem = pl.BlockSpec(memory_space=pltpu.SMEM)
    new_outer, new_moment, kv = pl.pallas_call(
        functools.partial(kernel, slots),
        out_shape=(
            jax.ShapeDtypeStruct((ROWS, WIDTH), F32),
            jax.ShapeDtypeStruct((ROWS, WIDTH), BF16),
            jax.ShapeDtypeStruct((TOKENS, WIDTH), BF16),
        ),
        in_specs=[smem, hbm, hbm, hbm, hbm, vmem, vmem, vmem, vmem],
        out_specs=(hbm, hbm, hbm),
        scratch_shapes=[
            pltpu.VMEM((CHUNKS, ROWS, CW), F32),
            pltpu.VMEM((CHUNKS, ROWS, CW), BF16),
            pltpu.VMEM((CHUNKS, ROWS, CW), BF16),
            pltpu.VMEM((TOKENS, DEPTH), BF16),
            pltpu.VMEM((CHUNKS, 4, 2, GROUP, CW), BF16),
            pltpu.VMEM((CHUNKS, 8 + slots, 2, GROUP, CW), BF16),
            pltpu.VMEM((CHUNKS if slots < 8 else 1, slots, 2, GROUP, CW), BF16),
            pltpu.VMEM((CHUNKS, 8, 2, GROUP, CW), BF16),
            pltpu.VMEM((CHUNKS, 4, 2, GROUP, CW), BF16),
            pltpu.VMEM((CHUNKS, DEPTH, CW), BF16),
            pltpu.VMEM((CHUNKS, TOKENS, CW), BF16),
            pltpu.SemaphoreType.DMA((9, CHUNKS)),
            pltpu.SemaphoreType.DMA((4, CHUNKS)),
            pltpu.SemaphoreType.DMA((5, CHUNKS)),
            pltpu.SemaphoreType.DMA((1,)),
        ],
        compiler_params=pltpu.CompilerParams(
            collective_id=0, has_side_effects=True, vmem_limit_bytes=62 * 2**20
        ),
    )(
        table,
        outer_weight[0],
        inner_weight[0],
        momentum[0],
        tokens[0],
        norm_gain,
        kv_bias,
        cosine,
        sine,
    )
    return (new_outer[None], new_moment[None], kv[None])


def solution(mesh):
    in_specs = (
        P("replica", "shard", None),
        P("replica", "shard", None),
        P("replica", "shard", None),
        P(),
        P("replica", "shard", None),
        P("replica", None),
        P("replica", None),
    )
    out_specs = (
        P("replica", "shard", None),
        P("replica", "shard", None),
        P("replica", "shard", None),
    )
    return jax.shard_map(on_device, mesh=mesh, in_specs=in_specs, out_specs=out_specs, check_vma=False)
```

time: 512 us -> 222 us (0.43); the launches traced: 503 us -> 222 us
  waiting for transfers between devices: 237 us -> 0 us
  Pallas kernels: 0 us -> 211 us
  other arithmetic: 98.2 us -> 3.74 us
  local copies, waits for them, and re-layouts: 84.9 us -> 6.31 us
  blocking collectives: 37.2 us -> 0 us
  starting transfers between devices: 21.1 us -> 0 us
  between operations: 14.6 us -> 0.68 us
  matrix products: 10.7 us -> 0 us
    pallas_call x0 -> x1, Pallas kernels: none -> 211 us  [on_device(): pl.pallas_call(functools.partial(kernel, slots), out_shape=(jax.ShapeDtyp...]
    all_gather x1 -> x0, waiting for transfers between devices: 197 us -> none  [on_device(): lax.all_gather(updated.astype(jnp.bfloat16), 'shard', axis=0, tiled=True)]
    unnamed x4 -> x0, other arithmetic: 72.2 us -> none
    all_to_all x3 -> x0, waiting for transfers between devices: 40.4 us -> none  [the longest x1 27.5 us: on_device(): lax.all_to_all(pair_delta, 'replica', split_axis=0, concat_axis=2, tiled=...]
    all_to_all x1 -> x0, blocking collectives: 37.2 us -> none  [on_device(): lax.all_to_all(pair_outer, 'replica', split_axis=0, concat_axis=2, tiled=...]
    unnamed x33 -> x7, local copies, waits for them, and re-layouts: 34.6 us -> 6.31 us
    convert_element_type x8 -> x0, local copies, waits for them, and re-layouts: 27.8 us -> none  [the longest x1 7.81 us: on_device(): own_round = outer_rows.astype(jnp.bfloat16)]
    all_to_all x3 -> x0, starting transfers between devices: 20.9 us -> none  [the longest x1 9.53 us: on_device(): lax.all_to_all(own_delta[None], 'replica', split_axis=2, concat_axis=0, t...]
  transfers between devices with their start and end apart: 4 -> 0, of which waited for: 3 -> 0; matrix products, arithmetic and copies ran while one was open for 16% -> 0% of each run, Pallas kernels for 0% -> 0%
where the time goes in v1:
time: 222 us
  Pallas kernels  211 us (95%)
  local copies, waits for them, and re-layouts  6.31 us (3%)
  other arithmetic  3.74 us (2%)
    pallas_call x1, Pallas kernels, on_device(): pl.pallas_call(functools.partial(kernel, slots), out_shape=(jax.ShapeDtyp...  211 us
    unnamed x7, local copies, waits for them, and re-layouts  6.31 us

profile of v1, /device:TPU:1, one launch (start us, length us, event | category | flops | bytes accessed | tf_op | source)
XLA Modules:
  0.0 222.0 jit_solution(17304367485096410344)
XLA Ops:
  0.6 0.8 select_reduce_fusion.2
  1.4 0.8 select_reduce_fusion.1
  2.3 0.2 select_reduce_fusion
  2.5 0.5 compare_select_fusion.4.mate_ref
  3.0 0.5 fusion
  3.6 0.8 pad_maximum_fusion
  4.4 211.3 %shard_map.94 = (f32[320,2048]{1,0:T(8,128)}, bf16[320,2048]{1,0:T(8,128)(2,1)}, bf16[256,2048]{1,0:T(8,128)(2,1)}) custom-call(s32[16]{0:T(128)} %compare_select_fusion.4.mate_ref, f32[320,2048]{1,0:T(8,128)} %bitcast.7, bf16[320,2048]{1,0:T(8,128)(2,1)} %bitcast.10, bf16[320,2048]{1,0:T(8,128)(2,1)} %bitcast.11, bf16[256,5120]{1,0:T(8,128)(2,1)} %bitcast.8, ...), custom_call_target="tpu_custom_call" | custom-call | tf_op jit(solution)/shard_map/pallas_call | solution.py:415
  215.7 0.0 copy-start
  215.7 3.6 %copy.13 = f32[1,320,2048]{2,1,0:T(8,128)} copy(f32[1,320,2048]{2,1,0:T(8,128)} %bitcast.9) | data formatting | bytes 5242880
  219.4 0.0 copy-done
  219.4 0.0 copy-start.1
  219.4 1.1 copy.14
  220.4 0.6 copy-done.1
  221.1 1.0 copy.15
  (4 shorter events, 0.0 us)
Async XLA Ops:
  215.7 3.6 %copy-start = (bf16[320,2048]{1,0:T(8,128)(2,1)S(1)}, bf16[320,2048]{1,0:T(8,128)(2,1)}, u32[]{:S(2)}) copy-start(bf16[320,2048]{1,0:T(8,128)(2,1)} %get-tuple-element.7) | copy-start | bytes 3932164
  219.4 1.7 copy-start.1

commit v2 on v1

--- a/solution.py
+++ b/solution.py
@@ -198,7 +198,8 @@
 
     def average(n):
         taken(pool.at[n, pl.ds(8, slots)], recv.at[B, n])
-        mates = [mate_ref[side * 8 + k] for k in range(8)]
+        first = side * 8 + (0 if slots < 8 else 32)
+        mates = [mate_ref[first + k] for k in range(8)]
 
         def part(i, _):
             v = i // 5
@@ -392,27 +393,28 @@
     return jnp.sum(picked * matching[None, :], axis=1)
 
 
-def on_device(outer_weight, inner_weight, momentum, matching, tokens, norm_gain, kv_bias):
+def pair_tables(matching):
     partner = partner_table(matching)
     order = jnp.arange(16, dtype=jnp.int32)
     replica_of = (order % 4) * 4 + (order // 8) * 2 + (order // 4) % 2
-    mate = jnp.sum(jnp.where(replica_of[:, None] == jnp.arange(16)[None, :], partner[None, :], 0), axis=1)
+    mate = jnp.sum(jnp.where(replica_of[:, None] == order[None, :], partner[None, :], 0), axis=1)
     mate_item = (mate % 4) // 2 * 8 + (mate % 2) * 4 + mate // 4
-    same_side = mate_item // 8 == order // 8
-    table = jnp.where(same_side, mate_item % 8, 8 + mate_item % 8).astype(jnp.int32)
-
-    positions = (lax.axis_index("shard") * TOKENS + jnp.arange(TOKENS, dtype=jnp.int32)).astype(F32)
-    exponents = jnp.arange(HEAD_DIM // 2, dtype=F32) * (2.0 / HEAD_DIM)
-    angles = positions[:, None] * (rope_base ** (-exponents))[None, :]
-    cosine, sine = jnp.cos(angles), jnp.sin(angles)
-    cosine = jnp.concatenate([cosine, cosine], axis=1)
-    sine = jnp.concatenate([-sine, sine], axis=1)
-
-    slots = 8
+    crosses = (mate_item // 8 != order // 8).astype(jnp.int32)
+    ahead = (order[None, :] < order[:, None]) & (order[None, :] // 8 == order[:, None] // 8)
+    rank = jnp.sum(jnp.where(ahead, crosses[None, :], 0), axis=1)
+    mate_rank = jnp.sum(jnp.where(mate_item[:, None] == order[None, :], rank[None, :], 0), axis=1)
+    whole = mate_item % 8 + 8 * crosses
+    packed = jnp.where(crosses == 1, 8 + mate_rank, mate_item % 8)
+    taken = (rank[None, :] == order[:, None] % 8) & (crosses[None, :] == 1) & (order[None, :] // 8 == order[:, None] // 8)
+    listed = jnp.sum(jnp.where(taken, order[None, :] % 8, 0), axis=1)
+    return jnp.concatenate([packed, listed, whole]).astype(jnp.int32), jnp.sum(crosses) // 2
+
+
+def launch(slots, *operands):
     hbm = pl.BlockSpec(memory_space=pl.ANY)
     vmem = pl.BlockSpec(memory_space=pltpu.VMEM)
     smem = pl.BlockSpec(memory_space=pltpu.SMEM)
-    new_outer, new_moment, kv = pl.pallas_call(
+    return pl.pallas_call(
         functools.partial(kernel, slots),
         out_shape=(
             jax.ShapeDtypeStruct((ROWS, WIDTH), F32),
@@ -439,9 +441,24 @@
             pltpu.SemaphoreType.DMA((1,)),
         ],
         compiler_params=pltpu.CompilerParams(
-            collective_id=0, has_side_effects=True, vmem_limit_bytes=62 * 2**20
+            collective_id=slots, has_side_effects=True, vmem_limit_bytes=62 * 2**20
         ),
-    )(
+    )(*operands)
+
+
+def on_device(outer_weight, inner_weight, momentum, matching, tokens, norm_gain, kv_bias):
+    table, count = pair_tables(matching)
+
+    positions = (lax.axis_index("shard") * TOKENS + jnp.arange(TOKENS, dtype=jnp.int32)).astype(F32)
+    exponents = jnp.arange(HEAD_DIM // 2, dtype=F32) * (2.0 / HEAD_DIM)
+    angles = positions[:, None] * (rope_base ** (-exponents))[None, :]
+    cosine, sine = jnp.cos(angles), jnp.sin(angles)
+    cosine = jnp.concatenate([cosine, cosine], axis=1)
+    sine = jnp.concatenate([-sine, sine], axis=1)
+
+    new_outer, new_moment, kv = lax.switch(
+        jnp.clip((count - 3) // 2, 0, 2),
+        [functools.partial(launch, slots) for slots in (4, 6, 8)],
         table,
         outer_weight[0],
         inner_weight[0],

time: 222 us -> 198 us (0.89)
  Pallas kernels: 211 us -> 183 us
  between operations: 0.68 us -> 3.31 us
    pallas_call x1, Pallas kernels: 211 us -> 183 us  [launch(): pl.pallas_call(functools.partial(kernel, slots), out_shape=(jax.ShapeDtyp...]
    unnamed x7 -> x5, local copies, waits for them, and re-layouts: 6.31 us -> 6.2 us
where the time goes in v2:
time: 198 us; the launch traced here: 197 us
  Pallas kernels  183 us (92%)
  local copies, waits for them, and re-layouts  6.2 us (3%)
  other arithmetic  3.62 us (2%)
  between operations  3.31 us (2%)
    pallas_call x1, Pallas kernels, launch(): pl.pallas_call(functools.partial(kernel, slots), out_shape=(jax.ShapeDtyp...  183 us
    unnamed x5, local copies, waits for them, and re-layouts  6.2 us

profile of v2, /device:TPU:1, one launch (start us, length us, event | category | flops | bytes accessed | tf_op | source)
XLA Modules:
  0.0 196.6 jit_solution(18170470112939464514)
XLA Ops:
  0.6 0.8 select_reduce_fusion.5
  1.4 0.8 select_reduce_fusion.4
  2.3 0.2 select_reduce_fusion.3
  2.5 0.2 select_reduce_fusion.2
  2.7 0.2 select_reduce_fusion.1
  2.9 0.6 add_select_fusion
  6.2 0.1 pad_add_fusion
  6.2 0.5 fusion
  6.8 0.1 pad_maximum_fusion
  6.9 183.5 %conditional.1 = ((f32[320,2048]{1,0:T(8,128)}, bf16[320,2048]{1,0:T(8,128)(2,1)S(1)}, bf16[256,2048]{1,0:T(8,128)(2,1)})) conditional(s32[]{:T(128)} %clamp.3, (f32[1,320,2048]{2,1,0:T(8,128)}, bf16[1,320,2048]{2,1,0:T(8,128)(2,1)}, bf16[1,320,2048]{2,1,0:T(8,128)(2,1)}, bf16[1,256,5120]{2,1,0:T(8,128)(2,1)}, s32[48]{0:T(128)S(1)}, ...), branch_computations={%region_7.8_spmd, %region_8.9_spmd, %region_9.10_spmd} | conditional | bytes 8 | solution.py:459
  6.9 183.5 %branch_1_fun.1 = (f32[320,2048]{1,0:T(8,128)}, bf16[320,2048]{1,0:T(8,128)(2,1)S(1)}, bf16[256,2048]{1,0:T(8,128)(2,1)}) custom-call(s32[48]{0:T(128)S(1)} %get-tuple-element.90.mate_ref, f32[320,2048]{1,0:T(8,128)} %bitcast.16, bf16[320,2048]{1,0:T(8,128)(2,1)} %bitcast.22, bf16[320,2048]{1,0:T(8,128)(2,1)} %bitcast.25, bf16[256,5120]{1,0:T(8,128)(2,1)} %bitcast.19, ...), custom_call_target="tpu_custom_call" | custom-call | tf_op jit(solution)/shard_map/cond/branch_1_fun/pallas_call | solution.py:417
  190.4 3.5 %copy.22 = f32[1,320,2048]{2,1,0:T(8,128)} copy(f32[1,320,2048]{2,1,0:T(8,128)} %bitcast.27) | data formatting | bytes 5242880
  194.0 0.0 copy-start
  194.0 1.1 copy.23
  195.0 0.6 copy-done
  195.7 1.0 copy.24
  (7 shorter events, 0.1 us)
Async XLA Ops:
  194.0 1.7 copy-start

commit v3 on v2

--- a/solution.py
+++ b/solution.py
@@ -2,6 +2,7 @@
 
 import jax
 import jax.numpy as jnp
+import numpy as np
 from jax import lax
 from jax.experimental import pallas as pl
 from jax.experimental.pallas import tpu as pltpu
@@ -25,27 +26,29 @@
 DEPTH = 5120
 GROUP = ROWS // 4
 HALF = ROWS // 2
-CHUNKS = 8
+CHUNKS = 16
 CW = WIDTH // CHUNKS
 AHEAD = 2
 NORM_TICKS = 4
-
-A, B, C, D, X1, X2, F1, F2, K = range(9)
-SA, SB, SC, SW = range(4)
+DIRECT = True
+EDGE_AHEAD = 1
+LAGS = (1, 2, 4, 5, 6, 7)
+
+A, B, C, D, X1, X2, F1, F2, K, E = range(10)
+SA, SB, SC, SW, SE = range(5)
 LO, LI, OO, OM, OK = range(5)
 
 
 def kernel(
     slots,
-    mate_ref,
+    match_ref,
     outer_hbm,
     inner_hbm,
     moment_hbm,
     token_hbm,
-    gain_ref,
-    bias_ref,
-    cos_ref,
-    sin_ref,
+    gain_hbm,
+    bias_hbm,
+    turn_hbm,
     new_outer_hbm,
     new_moment_hbm,
     kv_hbm,
@@ -60,6 +63,12 @@
     pair,
     weights,
     kv,
+    gain_ref,
+    bias_ref,
+    turn_ref,
+    cos_ref,
+    sin_ref,
+    mate_ref,
     recv,
     send,
     local,
@@ -107,6 +116,13 @@
         return pltpu.make_async_copy(moment_hbm.at[:, cols(n)], moment.at[n], local.at[OM, n])
 
     token_load = pltpu.make_async_copy(token_hbm, normed, single.at[0])
+    small_loads = (
+        pltpu.make_async_copy(gain_hbm, gain_ref, single.at[1]),
+        pltpu.make_async_copy(bias_hbm, bias_ref, single.at[2]),
+        pltpu.make_async_copy(
+            turn_hbm.at[pl.ds(pl.multiple_of(s * TOKENS, TOKENS), TOKENS)], turn_ref, single.at[3]
+        ),
+    )
 
     def start_loads(n, _):
         for copy in loads(n):
@@ -115,6 +131,8 @@
 
     lax.fori_loop(0, CHUNKS, start_loads, 0)
     token_load.start()
+    for copy in small_loads:
+        copy.start()
 
     def start_moment(n, _):
         moment_load(n).start()
@@ -129,13 +147,13 @@
 
     for device in (to_core, to_right, to_left, to_far):
         greet(device)
+    for step in range(1, 4):
+        greet(place((y + step) % 4, zl, zh, x, core))
 
     @pl.when(is_hub)
     def _():
         for step in range(4):
             greet(place((y + step) % 4, edge, zh, x, core))
-        for step in range(1, 4):
-            greet(place((y + step) % 4, zl, zh, x, core))
         greet(place(y, far, zh, x, core))
         pl.semaphore_wait(barrier, 12)
 
@@ -143,8 +161,10 @@
     def _():
         for step in range(4):
             greet(place((y + step) % 4, hub_z, zh, x, core))
-        pl.semaphore_wait(barrier, 8)
-
+        pl.semaphore_wait(barrier, 11)
+
+    own_items = pl.ds((zl % 2) * 4, 4)
+    edge_items = pl.ds((edge % 2) * 4, 4)
     item = (zl % 2) * 4 + y
 
     def send_rows(n):
@@ -163,8 +183,9 @@
             to_y = (y + step) % 4
             src, dst = sent.at[n, to_y], pool.at[n, item]
             if step:
-                remote(src, dst, send.at[SA, n], recv.at[A, n], place(to_y, hub_z, zh, x, core))
-            else:
+                to_z = hub_z if DIRECT else zl
+                remote(src, dst, send.at[SA, n], recv.at[A, n], place(to_y, to_z, zh, x, core))
+            elif DIRECT:
 
                 @pl.when(is_hub)
                 def _():
@@ -173,9 +194,20 @@
                 @pl.when(jnp.logical_not(is_hub))
                 def _():
                     remote(src, dst, send.at[SA, n], recv.at[A, n], place(to_y, hub_z, zh, x, core))
+            else:
+                pltpu.make_async_copy(src, dst, recv.at[A, n]).start()
+
+    def to_hub(n):
+        taken(pool.at[n, own_items], recv.at[A, n])
+        items = pool.at[n, own_items]
+        remote(items, items, send.at[SE, n], recv.at[E, n], place(y, hub_z, zh, x, core))
 
     def swap_sides(n):
-        taken(pool.at[n, pl.ds(0, 8)], recv.at[A, n])
+        if DIRECT:
+            taken(pool.at[n, pl.ds(0, 8)], recv.at[A, n])
+        else:
+            taken(pool.at[n, own_items], recv.at[A, n])
+            taken(pool.at[n, edge_items], recv.at[E, n])
         if slots < 8:
 
             def part(i, _):
@@ -183,7 +215,7 @@
                 rows = pl.ds(pl.multiple_of((i % 5) * 16, 16), 16)
                 held = [pool[n, j, v, rows, :] for j in range(8)]
                 for k in range(slots):
-                    which = mate_ref[16 + side * 8 + k]
+                    which = mate_ref[8 + k]
                     value = held[0]
                     for j in range(1, 8):
                         value = jnp.where(which == j, held[j], value)
@@ -198,8 +230,7 @@
 
     def average(n):
         taken(pool.at[n, pl.ds(8, slots)], recv.at[B, n])
-        first = side * 8 + (0 if slots < 8 else 32)
-        mates = [mate_ref[first + k] for k in range(8)]
+        mates = [mate_ref[k] for k in range(8)]
 
         def part(i, _):
             v = i // 5
@@ -298,6 +329,13 @@
         @pl.when(t == 0)
         def _():
             token_load.wait()
+            for copy in small_loads:
+                copy.wait()
+            turns = turn_ref[...]
+            swapped = pltpu.roll(turns, HEAD_DIM // 2, 1)
+            first = lax.broadcasted_iota(jnp.int32, turns.shape, 1) < HEAD_DIM // 2
+            cos_ref[...] = jnp.where(first, turns, swapped)
+            sin_ref[...] = jnp.where(first, -swapped, turns)
 
         per_tick = TOKENS // NORM_TICKS
 
@@ -327,16 +365,65 @@
 
         kv_store(n).start()
 
+    def find_mates():
+        found = [match_ref[p] for p in range(16)]
+
+        def mate_of(on_side, k):
+            replica = (k % 4) * 4 + on_side * 2 + k // 4
+            mate = 0
+            for p in range(16):
+                mate = mate + jnp.where(found[p] == replica, found[p ^ 1], 0)
+            crosses = jnp.where((mate // 2) % 2 != on_side, 1, 0)
+            return (mate % 2) * 4 + mate // 4, crosses
+
+        def ranks(crosses):
+            return [sum(crosses[:k], 0) for k in range(8)]
+
+        mates, crosses = zip(*[mate_of(side, k) for k in range(8)])
+        if slots == 8:
+            for k in range(8):
+                mate_ref[k] = mates[k] + 8 * crosses[k]
+            return
+        rank = ranks(crosses)
+        far_rank = ranks([mate_of(1 - side, k)[1] for k in range(8)])
+        for k in range(8):
+            place_far = 8
+            for j in range(8):
+                place_far = place_far + jnp.where(mates[k] == j, far_rank[j], 0)
+            mate_ref[k] = jnp.where(crosses[k] == 1, place_far, mates[k])
+        for slot in range(slots):
+            which = 0
+            for k in range(8):
+                which = which + jnp.where(jnp.logical_and(crosses[k] == 1, rank[k] == slot), k, 0)
+            mate_ref[8 + slot] = which
+
     def first_rows(n, _):
         send_rows(n)
         return 0
 
     lax.fori_loop(0, AHEAD, first_rows, 0)
 
+    @pl.when(is_hub)
+    def _():
+        find_mates()
+
+    if not DIRECT:
+
+        @pl.when(jnp.logical_not(is_hub))
+        def _():
+            for n in range(EDGE_AHEAD):
+                to_hub(n)
+
     def tick(t, _):
         @pl.when(t + AHEAD < CHUNKS)
         def _():
             send_rows(t + AHEAD)
+
+        if not DIRECT:
+
+            @pl.when(jnp.logical_and(jnp.logical_not(is_hub), t + EDGE_AHEAD < CHUNKS))
+            def _():
+                to_hub(t + EDGE_AHEAD)
 
         @pl.when(jnp.logical_and(is_hub, t < CHUNKS))
         def _():
@@ -353,15 +440,15 @@
             def _():
                 stage(t - lag)
 
-        staged(1, average, is_hub)
-        staged(2, update)
-        staged(3, first_hop)
-        staged(4, second_hop)
-        staged(5, third_hop)
-        staged(6, project)
+        staged(LAGS[0], average, is_hub)
+        staged(LAGS[1], update)
+        staged(LAGS[2], first_hop)
+        staged(LAGS[3], second_hop)
+        staged(LAGS[4], third_hop)
+        staged(LAGS[5], project)
         return 0
 
-    lax.fori_loop(0, CHUNKS + 6, tick, 0)
+    lax.fori_loop(0, CHUNKS + LAGS[5], tick, 0)
 
     def drain(n, _):
         @pl.when(is_hub)
@@ -372,7 +459,11 @@
 
         @pl.when(jnp.logical_not(is_hub))
         def _():
-            taken(sent.at[n], send.at[SA, n])
+            if DIRECT:
+                taken(sent.at[n], send.at[SA, n])
+            else:
+                taken(sent.at[n, pl.ds(0, 3)], send.at[SA, n])
+                taken(pool.at[n, own_items], send.at[SE, n])
 
         taken(weights.at[n, pl.ds(0, 15 * ROWS)], send.at[SW, n])
         outer_store(n).wait()
@@ -383,36 +474,16 @@
     lax.fori_loop(0, CHUNKS, drain, 0)
 
 
-def partner_table(matching):
-    total_count = matching.shape[0]
-    indices = jnp.arange(total_count, dtype=jnp.int32)
-    matches = (matching[None, :] == indices[:, None]).astype(jnp.int32)
-    position = jnp.sum(matches * indices[None, :], axis=1)
-    mate_pos = position + 1 - 2 * (position % 2)
-    picked = (indices[None, :] == mate_pos[:, None]).astype(jnp.int32)
-    return jnp.sum(picked * matching[None, :], axis=1)
-
-
-def pair_tables(matching):
-    partner = partner_table(matching)
-    order = jnp.arange(16, dtype=jnp.int32)
-    replica_of = (order % 4) * 4 + (order // 8) * 2 + (order // 4) % 2
-    mate = jnp.sum(jnp.where(replica_of[:, None] == order[None, :], partner[None, :], 0), axis=1)
-    mate_item = (mate % 4) // 2 * 8 + (mate % 2) * 4 + mate // 4
-    crosses = (mate_item // 8 != order // 8).astype(jnp.int32)
-    ahead = (order[None, :] < order[:, None]) & (order[None, :] // 8 == order[:, None] // 8)
-    rank = jnp.sum(jnp.where(ahead, crosses[None, :], 0), axis=1)
-    mate_rank = jnp.sum(jnp.where(mate_item[:, None] == order[None, :], rank[None, :], 0), axis=1)
-    whole = mate_item % 8 + 8 * crosses
-    packed = jnp.where(crosses == 1, 8 + mate_rank, mate_item % 8)
-    taken = (rank[None, :] == order[:, None] % 8) & (crosses[None, :] == 1) & (order[None, :] // 8 == order[:, None] // 8)
-    listed = jnp.sum(jnp.where(taken, order[None, :] % 8, 0), axis=1)
-    return jnp.concatenate([packed, listed, whole]).astype(jnp.int32), jnp.sum(crosses) // 2
+def turn_table(tokens):
+    exponents = np.arange(HEAD_DIM // 2, dtype=np.float32) * np.float32(2.0 / HEAD_DIM)
+    inverse = (rope_base ** (-exponents.astype(np.float64))).astype(np.float32)
+    angles = np.arange(tokens, dtype=np.float32)[:, None] * inverse[None, :]
+    angles = angles.astype(np.float64)
+    return np.concatenate([np.cos(angles), np.sin(angles)], axis=1).astype(np.float32)
 
 
 def launch(slots, *operands):
     hbm = pl.BlockSpec(memory_space=pl.ANY)
-    vmem = pl.BlockSpec(memory_space=pltpu.VMEM)
     smem = pl.BlockSpec(memory_space=pltpu.SMEM)
     return pl.pallas_call(
         functools.partial(kernel, slots),
@@ -421,7 +492,7 @@
             jax.ShapeDtypeStruct((ROWS, WIDTH), BF16),
             jax.ShapeDtypeStruct((TOKENS, WIDTH), BF16),
         ),
-        in_specs=[smem, hbm, hbm, hbm, hbm, vmem, vmem, vmem, vmem],
+        in_specs=[smem] + [hbm] * 7,
         out_specs=(hbm, hbm, hbm),
         scratch_shapes=[
             pltpu.VMEM((CHUNKS, ROWS, CW), F32),
@@ -435,10 +506,16 @@
             pltpu.VMEM((CHUNKS, 4, 2, GROUP, CW), BF16),
             pltpu.VMEM((CHUNKS, DEPTH, CW), BF16),
             pltpu.VMEM((CHUNKS, TOKENS, CW), BF16),
-            pltpu.SemaphoreType.DMA((9, CHUNKS)),
-            pltpu.SemaphoreType.DMA((4, CHUNKS)),
+            pltpu.VMEM((1, DEPTH), F32),
+            pltpu.VMEM((1, WIDTH), F32),
+            pltpu.VMEM((TOKENS, HEAD_DIM), F32),
+            pltpu.VMEM((TOKENS, HEAD_DIM), F32),
+            pltpu.VMEM((TOKENS, HEAD_DIM), F32),
+            pltpu.SMEM((16,), jnp.int32),
+            pltpu.SemaphoreType.DMA((10, CHUNKS)),
             pltpu.SemaphoreType.DMA((5, CHUNKS)),
-            pltpu.SemaphoreType.DMA((1,)),
+            pltpu.SemaphoreType.DMA((5, CHUNKS)),
+            pltpu.SemaphoreType.DMA((4,)),
         ],
         compiler_params=pltpu.CompilerParams(
             collective_id=slots, has_side_effects=True, vmem_limit_bytes=62 * 2**20
@@ -447,27 +524,21 @@
 
 
 def on_device(outer_weight, inner_weight, momentum, matching, tokens, norm_gain, kv_bias):
-    table, count = pair_tables(matching)
-
-    positions = (lax.axis_index("shard") * TOKENS + jnp.arange(TOKENS, dtype=jnp.int32)).astype(F32)
-    exponents = jnp.arange(HEAD_DIM // 2, dtype=F32) * (2.0 / HEAD_DIM)
-    angles = positions[:, None] * (rope_base ** (-exponents))[None, :]
-    cosine, sine = jnp.cos(angles), jnp.sin(angles)
-    cosine = jnp.concatenate([cosine, cosine], axis=1)
-    sine = jnp.concatenate([-sine, sine], axis=1)
+    sides = (matching // 2) % 2
+    count = jnp.sum(sides.reshape(8, 2)[:, 0] != sides.reshape(8, 2)[:, 1])
+    turns = jnp.asarray(turn_table(TOKENS * lax.axis_size("shard")))
 
     new_outer, new_moment, kv = lax.switch(
         jnp.clip((count - 3) // 2, 0, 2),
         [functools.partial(launch, slots) for slots in (4, 6, 8)],
-        table,
+        matching,
         outer_weight[0],
         inner_weight[0],
         momentum[0],
         tokens[0],
         norm_gain,
         kv_bias,
-        cosine,
-        sine,
+        turns,
     )
     return (new_outer[None], new_moment[None], kv[None])
 

time: 198 us -> 192 us (0.970)
  other arithmetic: 3.62 us -> 1.38 us
  between operations: 3.31 us -> 1.32 us
where the time goes in v3:
time: 192 us
  Pallas kernels  183 us (95%)
  local copies, waits for them, and re-layouts  6.28 us (3%)
    pallas_call x1, Pallas kernels, launch(): pl.pallas_call(functools.partial(kernel, slots), out_shape=(jax.ShapeDtyp...  183 us
    unnamed x5, local copies, waits for them, and re-layouts  6.2 us

profile of v3, /device:TPU:1, one launch (start us, length us, event | category | flops | bytes accessed | tf_op | source)
XLA Modules:
  0.0 191.8 jit_solution(12758433068066785118)
XLA Ops:
  0.6 0.7 and_select_fusion
  1.3 0.1 reshape.12
  1.4 0.7 convert_reduce_fusion
  2.8 182.8 %conditional.1 = ((f32[320,2048]{1,0:T(8,128)}, bf16[320,2048]{1,0:T(8,128)(2,1)S(1)}, bf16[256,2048]{1,0:T(8,128)(2,1)})) conditional(s32[]{:T(128)} %clamp.3, (s32[16]{0:T(128)}, f32[320,2048]{1,0:T(8,128)}, bf16[320,2048]{1,0:T(8,128)(2,1)}, bf16[320,2048]{1,0:T(8,128)(2,1)}, bf16[256,5120]{1,0:T(8,128)(2,1)}, ...), branch_computations={%region_1.2_spmd, %region_2.3_spmd, %region_3.4_spmd} | conditional | bytes 8 | solution.py:531
  2.8 182.7 %branch_1_fun.1 = (f32[320,2048]{1,0:T(8,128)}, bf16[320,2048]{1,0:T(8,128)(2,1)S(1)}, bf16[256,2048]{1,0:T(8,128)(2,1)}) custom-call(s32[16]{0:T(128)} %get-tuple-element.71.match_ref, f32[320,2048]{1,0:T(8,128)} %get-tuple-element.72.outer_hbm, bf16[320,2048]{1,0:T(8,128)(2,1)} %get-tuple-element.73.inner_hbm, ...), custom_call_target="tpu_custom_call" | custom-call | tf_op jit(solution)/shard_map/cond/branch_1_fun/pallas_call | solution.py:488
  185.6 3.5 %copy.23 = f32[1,320,2048]{2,1,0:T(8,128)} copy(f32[1,320,2048]{2,1,0:T(8,128)} %bitcast.19) | data formatting | bytes 5242880
  189.1 0.0 copy-start
  189.1 1.1 copy.24
  190.1 0.6 copy-done
  190.8 1.0 copy.25
Async XLA Ops:
  189.1 1.7 copy-start

commit v4 on v3

--- a/solution.py
+++ b/solution.py
@@ -523,9 +523,40 @@
     )(*operands)
 
 
+def copy_kernel(*refs):
+    sems = refs[-1]
+    loads, stores = [], []
+    for src, dst, held, parts in zip(refs[:3], refs[3:6], refs[6:9], (8, 4, 4)):
+        size = src.shape[0] // parts
+        for i in range(parts):
+            rows, j = pl.ds(i * size, size), len(loads)
+            loads.append(pltpu.make_async_copy(src.at[rows], held.at[rows], sems.at[0, j]))
+            stores.append(pltpu.make_async_copy(held.at[rows], dst.at[rows], sems.at[1, j]))
+    for load in loads:
+        load.start()
+    for load, store in zip(loads, stores):
+        load.wait()
+        store.start()
+    for store in stores:
+        store.wait()
+
+
+def copied(*arrays):
+    hbm = pl.BlockSpec(memory_space=pl.ANY)
+    return pl.pallas_call(
+        copy_kernel,
+        out_shape=tuple(jax.ShapeDtypeStruct(a.shape, a.dtype) for a in arrays),
+        in_specs=[hbm] * 3,
+        out_specs=(hbm,) * 3,
+        scratch_shapes=[pltpu.VMEM(a.shape, a.dtype) for a in arrays] + [pltpu.SemaphoreType.DMA((2, 16))],
+        compiler_params=pltpu.CompilerParams(vmem_limit_bytes=16 * 2**20),
+    )(*arrays)
+
+
 def on_device(outer_weight, inner_weight, momentum, matching, tokens, norm_gain, kv_bias):
-    sides = (matching // 2) % 2
-    count = jnp.sum(sides.reshape(8, 2)[:, 0] != sides.reshape(8, 2)[:, 1])
+    order = jnp.arange(16, dtype=jnp.int32)
+    paired = (order[None, :] == order[:, None] + 1) & (order[:, None] % 2 == 0)
+    count = jnp.sum(jnp.where(paired, ((matching[None, :] ^ matching[:, None]) >> 1) & 1, 0))
     turns = jnp.asarray(turn_table(TOKENS * lax.axis_size("shard")))
 
     new_outer, new_moment, kv = lax.switch(
@@ -540,6 +571,7 @@
         kv_bias,
         turns,
     )
+    new_outer, new_moment, kv = copied(new_outer, new_moment, kv)
     return (new_outer[None], new_moment[None], kv[None])
 
 

time: 192 us -> 164 us (0.85)
  Pallas kernels: 183 us -> 161 us
  local copies, waits for them, and re-layouts: 6.28 us -> 0 us
    pallas_call x1, Pallas kernels: 183 us -> 158 us  [launch(): pl.pallas_call(functools.partial(kernel, slots), out_shape=(jax.ShapeDtyp...]
    unnamed x5 -> x0, local copies, waits for them, and re-layouts: 6.2 us -> none
    pallas_call x0 -> x1, Pallas kernels: none -> 3.49 us  [copied(): pl.pallas_call(copy_kernel, out_shape=tuple((jax.ShapeDtypeStruct(a.shape...]
where the time goes in v4:
time: 164 us
  Pallas kernels  161 us (98%)
    pallas_call x1, Pallas kernels, launch(): pl.pallas_call(functools.partial(kernel, slots), out_shape=(jax.ShapeDtyp...  158 us
    pallas_call x1, Pallas kernels, copied(): pl.pallas_call(copy_kernel, out_shape=tuple((jax.ShapeDtypeStruct(a.shape...  3.49 us

profile of v4, /device:TPU:1, one launch (start us, length us, event | category | flops | bytes accessed | tf_op | source)
XLA Modules:
  0.0 164.1 jit_solution(16183283021444048847)
XLA Ops:
  0.7 1.4 select_reduce_fusion
  2.8 157.8 %conditional.1 = ((f32[320,2048]{1,0:T(8,128)}, bf16[320,2048]{1,0:T(8,128)(2,1)S(1)}, bf16[256,2048]{1,0:T(8,128)(2,1)})) conditional(s32[]{:T(128)} %clamp.3, (s32[16]{0:T(128)}, f32[320,2048]{1,0:T(8,128)}, bf16[320,2048]{1,0:T(8,128)(2,1)}, bf16[320,2048]{1,0:T(8,128)(2,1)}, bf16[256,5120]{1,0:T(8,128)(2,1)}, ...), branch_computations={%region_1.2_spmd, %region_2.3_spmd, %region_3.4_spmd} | conditional | bytes 8 | solution.py:562
  2.8 157.8 %branch_0_fun.1 = (f32[320,2048]{1,0:T(8,128)}, bf16[320,2048]{1,0:T(8,128)(2,1)S(1)}, bf16[256,2048]{1,0:T(8,128)(2,1)}) custom-call(s32[16]{0:T(128)} %get-tuple-element.48.match_ref, f32[320,2048]{1,0:T(8,128)} %get-tuple-element.49.outer_hbm, bf16[320,2048]{1,0:T(8,128)(2,1)} %get-tuple-element.50.inner_hbm, ...), custom_call_target="tpu_custom_call" | custom-call | tf_op jit(solution)/shard_map/cond/branch_0_fun/pallas_call | solution.py:488
  160.6 3.5 %shard_map.103 = (f32[320,2048]{1,0:T(8,128)}, bf16[320,2048]{1,0:T(8,128)(2,1)}, bf16[256,2048]{1,0:T(8,128)(2,1)}) custom-call(f32[320,2048]{1,0:T(8,128)} %get-tuple-element.81.refs_0_, bf16[320,2048]{1,0:T(8,128)(2,1)S(1)} %get-tuple-element.82.refs_1_, bf16[256,2048]{1,0:T(8,128)(2,1)} %get-tuple-element.83.refs_2_), custom_call_target="tpu_custom_call" | custom-call | tf_op jit(solution)/shard_map/pallas_call | solution.py:546
  (2 shorter events, 0.0 us)
